TPU v7x, 32 devices: a whole 2x2x4 slice. The times are simulated.
32 devices in a mesh: row: 2 (over x), blk: 16 (over z, y, core).
Axes of the slice: x: 2, y: 2, z: 4, core: 2. Of those that a mesh axis runs over, the one named last changes fastest.
Arguments:
- matrix: float32 [4096, 2048], P('row', 'blk'), may hold values from -72 to 72, as said below
- prior: float32 [2048, 2048], P('row', 'blk'), may hold values from -6 to 6
Outputs:
- turned: float32 [4096, 2048], P('row', 'blk')
- transform: float32 [2048, 2048], P('row', 'blk')
- off_ratio: float32 [8], replicated
Inputs may be any that keep to these rules, and one draw needn't show every extreme that they name: `matrix`: every column is nonzero.
All inputs are finite; a program needn't handle non-finite values.
Results may differ from a plain program's by a relative error of at most 0.0003.
Values sent between devices are 32-bit elements; how exact they have to be, the bound alone decides.
A program may use at most 64 MiB of HBM per device.

v0:
```python
import jax
import jax.numpy as jnp
from jax import lax
from jax.sharding import PartitionSpec as P

ROUNDS = 8
NS_STEPS = 8


HIGH = lax.Precision.HIGHEST


def passed_along(shard, axis, by):
    devices = lax.axis_size(axis)
    pairs = [(i, i + by) for i in range(devices) if 0 <= i + by < devices]
    return lax.ppermute(shard, axis, pairs)


def rotation(gram_sum):
    pair_width = gram_sum.shape[0]
    diag_vals = jnp.diagonal(gram_sum)
    weights = jnp.arange(pair_width, dtype=jnp.float32) / pair_width
    mean_diag = jnp.mean(diag_vals)
    skew_part = gram_sum * (weights[None, :] - weights[:, None]) / mean_diag
    factor = lax.rsqrt(1.0 + jnp.sum(skew_part * skew_part))
    identity = jnp.eye(pair_width, dtype=jnp.float32)
    rotator = (identity + skew_part) * factor
    for repeat in range(NS_STEPS):
        square = jnp.dot(rotator.T, rotator, precision=HIGH, preferred_element_type=jnp.float32)
        rotator = 1.5 * rotator - 0.5 * jnp.dot(
            rotator, square, precision=HIGH, preferred_element_type=jnp.float32
        )
    off_sq = jnp.sum(jnp.where(identity > 0.5, 0.0, gram_sum * gram_sum))
    diag_sq = jnp.sum(diag_vals * diag_vals)
    return (rotator, off_sq, diag_sq)


def send_up(stacked):
    return passed_along(stacked, "blk", 1)


def send_down(stacked):
    return passed_along(stacked, "blk", -1)


def body(matrix, prior):
    rows_local = matrix.shape[0]
    pair_width = matrix.shape[1]
    half_width = pair_width // 2
    blk_count = lax.axis_size("blk")
    blk_index = lax.axis_index("blk")
    stacked = jnp.concatenate([matrix, prior], axis=0)
    first_slot = blk_index == 0
    last_slot = blk_index == blk_count - 1
    off_list = []
    diag_list = []
    for round_index in range(ROUNDS):
        local_rows = stacked[:rows_local]
        partial_value = jnp.dot(
            local_rows.T, local_rows, precision=HIGH, preferred_element_type=jnp.float32
        )
        gram_sum = lax.psum(partial_value, "row")
        rotator, off_sq, diag_sq = rotation(gram_sum)
        rotated = jnp.dot(stacked, rotator, precision=HIGH, preferred_element_type=jnp.float32)
        top_turned = rotated[:, :half_width]
        bottom_turned = rotated[:, half_width:]
        from_below = send_up(jnp.where(first_slot, bottom_turned, top_turned))
        from_above = send_down(bottom_turned)
        new_top = jnp.where(first_slot, top_turned, from_below)
        new_bottom = jnp.where(last_slot, top_turned, from_above)
        stacked = jnp.concatenate([new_top, new_bottom], axis=1)
        off_list.append(off_sq)
        diag_list.append(diag_sq)
    off_totals, diag_totals = lax.psum((jnp.stack(off_list), jnp.stack(diag_list)), "blk")
    off_ratio = jnp.sqrt(off_totals / diag_totals)
    return (stacked[:rows_local], stacked[rows_local:], off_ratio)


def solution(mesh):
    return jax.shard_map(
        body,
        mesh=mesh,
        in_specs=(P("row", "blk"), P("row", "blk")),
        out_specs=(P("row", "blk"), P("row", "blk"), P()),
        check_vma=False,
    )
```

profile of v0, /device:TPU:0, one launch (start us, length us, event | category | flops | bytes accessed | tf_op | source)
XLA Modules:
  0.0 509.3 jit_solution(11872230362361563004)
XLA Ops:
  7.2 4.0 fusion.213
  11.3 23.5 %all-reduce.10.cloned.1.call-done = f32[128,128]{1,0:T(8,128)} async-done(((f32[128,128]{1,0:T(8,128)}), f32[128,128]{1,0:T(8,128)}) %all-reduce.10.cloned.1.call-update) | async-done | bytes 65552 | tf_op jit(solution)/shard_map/psum | solution.py:62
  34.8 1.9 gather_fusion
  53.3 3.0 collective-permute-done.1
  57.7 1.6 fusion.121
  59.8 35.2 %all-reduce.12.cloned.1.call-done = f32[128,128]{1,0:T(8,128)} async-done(((f32[128,128]{1,0:T(8,128)}), f32[128,128]{1,0:T(8,128)}) %all-reduce.12.cloned.1.call-update) | async-done | bytes 65552 | tf_op jit(solution)/shard_map/psum | solution.py:62
  95.1 1.9 gather_fusion.1
  111.4 4.0 collective-permute-done.3
  117.2 34.9 %all-reduce.14.cloned.1.call-done = f32[128,128]{1,0:T(8,128)} async-done(((f32[128,128]{1,0:T(8,128)}), f32[128,128]{1,0:T(8,128)}) %all-reduce.14.cloned.1.call-update) | async-done | bytes 65552 | tf_op jit(solution)/shard_map/psum | solution.py:62
  152.1 1.9 gather_fusion.2
  168.5 4.0 collective-permute-done.5
  172.6 1.6 fusion.113
  174.3 34.9 %all-reduce.16.cloned.1.call-done = f32[128,128]{1,0:T(8,128)} async-done(((f32[128,128]{1,0:T(8,128)}), f32[128,128]{1,0:T(8,128)}) %all-reduce.16.cloned.1.call-update) | async-done | bytes 65552 | tf_op jit(solution)/shard_map/psum | solution.py:62
  209.2 1.9 gather_fusion.3
  225.6 4.0 collective-permute-done.7
  229.7 1.6 fusion.109
  231.4 34.9 %all-reduce.18.cloned.1.call-done = f32[128,128]{1,0:T(8,128)} async-done(((f32[128,128]{1,0:T(8,128)}), f32[128,128]{1,0:T(8,128)}) %all-reduce.18.cloned.1.call-update) | async-done | bytes 65552 | tf_op jit(solution)/shard_map/psum | solution.py:62
  266.3 1.9 gather_fusion.4
  282.6 4.0 collective-permute-done.9
  286.8 1.6 fusion.105
  288.4 34.9 %all-reduce.20.cloned.1.call-done = f32[128,128]{1,0:T(8,128)} async-done(((f32[128,128]{1,0:T(8,128)}), f32[128,128]{1,0:T(8,128)}) %all-reduce.20.cloned.1.call-update) | async-done | bytes 65552 | tf_op jit(solution)/shard_map/psum | solution.py:62
  323.3 1.9 gather_fusion.5
  339.7 4.0 collective-permute-done.11
  345.5 34.9 %all-reduce.22.cloned.1.call-done = f32[128,128]{1,0:T(8,128)} async-done(((f32[128,128]{1,0:T(8,128)}), f32[128,128]{1,0:T(8,128)}) %all-reduce.22.cloned.1.call-update) | async-done | bytes 65552 | tf_op jit(solution)/shard_map/psum | solution.py:62
  380.4 1.9 gather_fusion.6
  396.8 4.2 collective-permute-done.13
  402.8 34.7 %all-reduce.24.cloned.1.call-done = f32[128,128]{1,0:T(8,128)} async-done(((f32[128,128]{1,0:T(8,128)}), f32[128,128]{1,0:T(8,128)}) %all-reduce.24.cloned.1.call-update) | async-done | bytes 65552 | tf_op jit(solution)/shard_map/psum | solution.py:62
  437.4 1.9 gather_fusion.7
  453.0 3.1 collective-permute-start.14
  456.1 5.2 %stack.71 = f32[8]{0:T(128)S(1)} concatenate(f32[1]{0:T(128)} %bitcast.9, f32[1]{0:T(128)} %bitcast.10, f32[1]{0:T(128)} %bitcast.11, f32[1]{0:T(128)} %bitcast.12, f32[1]{0:T(128)} %bitcast.13, f32[1]{0:T(128)} %bitcast.14, f32[1]{0:T(128)} %bitcast.15, f32[1]{0:T(128)} %bitcast.16), dimensions={0} | concatenate | bytes 64 | tf_op jit(solution)/shard_map/stack | solution.py:74
  461.2 4.9 stack.62
  466.2 32.7 %all-reduce = (f32[8]{0:T(128)S(1)}, f32[8]{0:T(128)S(1)}) all-reduce(f32[8]{0:T(128)S(1)} %stack.62, f32[8]{0:T(128)S(1)} %stack.71), channel_id=1, replica_groups=mesh['row'=2,'blk'=16] {'blk'}, use_global_device_ids=true, to_apply=%region_32.33 | all-reduce | flops 16 | bytes 128 | tf_op jit(solution)/shard_map/psum | solution.py:74
  (224 shorter events, 115.8 us)
Async XLA Ops:
  7.2 27.7 %all-reduce.10.cloned.1.call-start = ((), (), s32[]{:S(2)}) async-start(), calls=%async_computation | async-start | bytes 131072 | tf_op jit(solution)/shard_map/psum | solution.py:62
  11.2 83.8 %all-reduce.12.cloned.1.call-start = ((), (), s32[]{:S(2)}) async-start(), calls=%async_computation.1 | async-start | bytes 131072 | tf_op jit(solution)/shard_map/psum | solution.py:62
  41.6 4.8 copy-start
  41.6 4.8 copy-start.2
  49.0 3.4 collective-permute-start
  50.4 5.9 %collective-permute-start.1 = (f32[3072,64]{0,1:T(8,128)S(1)}, f32[3072,64]{0,1:T(8,128)}, u32[]{:S(2)}, u32[]{:S(2)}) collective-permute-start(f32[3072,64]{0,1:T(8,128)S(1)} %get-tuple-element.74), channel_id=1, source_target_pairs={{1,0},{2,1},{3,2},{4,3},{5,4},{6,5},{7,6},{8,7},{9,8},{10,9},{11,1... | collective-permute-start | bytes 2359304 | tf_op jit(solution)/shard_map/ppermute | solution.py:16
  52.4 0.9 copy-start.1
  59.3 92.8 %all-reduce.14.cloned.1.call-start = ((), (), s32[]{:S(2)}) async-start(), calls=%async_computation.2 | async-start | bytes 131072 | tf_op jit(solution)/shard_map/psum | solution.py:62
  108.2 3.2 collective-permute-start.2
  109.6 5.8 %collective-permute-start.3 = (f32[3072,64]{0,1:T(8,128)S(1)}, f32[3072,64]{0,1:T(8,128)S(1)}, u32[]{:S(2)}, u32[]{:S(2)}) collective-permute-start(f32[3072,64]{0,1:T(8,128)S(1)} %get-tuple-element.70), channel_id=1, source_target_pairs={{1,0},{2,1},{3,2},{4,3},{5,4},{6,5},{7,6},{8,7},{9,8},{10,9},{11,1... | collective-permute-start | bytes 2359304 | tf_op jit(solution)/shard_map/ppermute | solution.py:16
  117.2 92.0 %all-reduce.16.cloned.1.call-start = ((), (), s32[]{:S(2)}) async-start(), calls=%async_computation.3 | async-start | bytes 131072 | tf_op jit(solution)/shard_map/psum | solution.py:62
  165.3 3.2 collective-permute-start.4
  166.7 5.8 %collective-permute-start.5 = (f32[3072,64]{0,1:T(8,128)S(1)}, f32[3072,64]{0,1:T(8,128)S(1)}, u32[]{:S(2)}, u32[]{:S(2)}) collective-permute-start(f32[3072,64]{0,1:T(8,128)S(1)} %get-tuple-element.66), channel_id=1, source_target_pairs={{1,0},{2,1},{3,2},{4,3},{5,4},{6,5},{7,6},{8,7},{9,8},{10,9},{11,1... | collective-permute-start | bytes 2359304 | tf_op jit(solution)/shard_map/ppermute | solution.py:16
  174.3 92.0 %all-reduce.18.cloned.1.call-start = ((), (), s32[]{:S(2)}) async-start(), calls=%async_computation.4 | async-start | bytes 131072 | tf_op jit(solution)/shard_map/psum | solution.py:62
  222.4 3.2 collective-permute-start.6
  223.7 5.8 %collective-permute-start.7 = (f32[3072,64]{0,1:T(8,128)S(1)}, f32[3072,64]{0,1:T(8,128)S(1)}, u32[]{:S(2)}, u32[]{:S(2)}) collective-permute-start(f32[3072,64]{0,1:T(8,128)S(1)} %get-tuple-element.62), channel_id=1, source_target_pairs={{1,0},{2,1},{3,2},{4,3},{5,4},{6,5},{7,6},{8,7},{9,8},{10,9},{11,1... | collective-permute-start | bytes 2359304 | tf_op jit(solution)/shard_map/ppermute | solution.py:16
  231.3 92.0 %all-reduce.20.cloned.1.call-start = ((), (), s32[]{:S(2)}) async-start(), calls=%async_computation.5 | async-start | bytes 131072 | tf_op jit(solution)/shard_map/psum | solution.py:62
  279.4 3.2 collective-permute-start.8
  280.8 5.8 %collective-permute-start.9 = (f32[3072,64]{0,1:T(8,128)S(1)}, f32[3072,64]{0,1:T(8,128)S(1)}, u32[]{:S(2)}, u32[]{:S(2)}) collective-permute-start(f32[3072,64]{0,1:T(8,128)S(1)} %get-tuple-element.58), channel_id=1, source_target_pairs={{1,0},{2,1},{3,2},{4,3},{5,4},{6,5},{7,6},{8,7},{9,8},{10,9},{11,1... | collective-permute-start | bytes 2359304 | tf_op jit(solution)/shard_map/ppermute | solution.py:16
  288.4 92.0 %all-reduce.22.cloned.1.call-start = ((), (), s32[]{:S(2)}) async-start(), calls=%async_computation.6 | async-start | bytes 131072 | tf_op jit(solution)/shard_map/psum | solution.py:62
  336.5 3.2 collective-permute-start.10
  337.9 5.8 %collective-permute-start.11 = (f32[3072,64]{0,1:T(8,128)S(1)}, f32[3072,64]{0,1:T(8,128)S(1)}, u32[]{:S(2)}, u32[]{:S(2)}) collective-permute-start(f32[3072,64]{0,1:T(8,128)S(1)} %get-tuple-element.54), channel_id=1, source_target_pairs={{1,0},{2,1},{3,2},{4,3},{5,4},{6,5},{7,6},{8,7},{9,8},{10,9},{11,1... | collective-permute-start | bytes 2359304 | tf_op jit(solution)/shard_map/ppermute | solution.py:16
  345.5 92.0 %all-reduce.24.cloned.1.call-start = ((), (), s32[]{:S(2)}) async-start(), calls=%async_computation.7 | async-start | bytes 131072 | tf_op jit(solution)/shard_map/psum | solution.py:62
  393.6 3.2 collective-permute-start.12
  395.2 5.8 %collective-permute-start.13 = (f32[3072,64]{0,1:T(8,128)S(1)}, f32[3072,64]{0,1:T(8,128)S(1)}, u32[]{:S(2)}, u32[]{:S(2)}) collective-permute-start(f32[3072,64]{0,1:T(8,128)S(1)} %get-tuple-element.50), channel_id=1, source_target_pairs={{1,0},{2,1},{3,2},{4,3},{5,4},{6,5},{7,6},{8,7},{9,8},{10,9},{11,1... | collective-permute-start | bytes 2359304 | tf_op jit(solution)/shard_map/ppermute | solution.py:16
  451.7 47.7 %collective-permute-start.15 = (f32[3072,64]{0,1:T(8,128)}, f32[3072,64]{0,1:T(8,128)S(1)}, u32[]{:S(2)}, u32[]{:S(2)}) collective-permute-start(f32[3072,64]{0,1:T(8,128)} %get-tuple-element.45), channel_id=1, source_target_pairs={{1,0},{2,1},{3,2},{4,3},{5,4},{6,5},{7,6},{8,7},{9,8},{10,9},{11,1... | collective-permute-start | bytes 2359304 | tf_op jit(solution)/shard_map/ppermute | solution.py:16
  453.0 46.4 %collective-permute-start.14 = (f32[3072,64]{0,1:T(8,128)}, f32[3072,64]{0,1:T(8,128)S(1)}, u32[]{:S(2)}, u32[]{:S(2)}) collective-permute-start(f32[3072,64]{0,1:T(8,128)} %get-tuple-element.46), channel_id=1, source_target_pairs={{0,1},{1,2},{2,3},{3,4},{4,5},{5,6},{6,7},{7,8},{8,9},{9,10},{10,1... | collective-permute-start | bytes 2359304 | tf_op jit(solution)/shard_map/ppermute | solution.py:16
Sparse Core Ops, SparseCore 0:
  11.3 23.4 all-reduce.9
  59.4 35.5 all-reduce.11
  117.3 34.7 all-reduce.13
  174.4 34.7 all-reduce.15
  231.5 34.7 all-reduce.17
  288.5 34.7 all-reduce.19
  345.6 34.7 all-reduce.21
  402.9 34.5 all-reduce.23
where the time goes:
time: 517 us; the launch traced here: 509 us
  waiting for transfers between devices  298 us (58%)
  matrix products  74.7 us (14%)
  blocking collectives  32.7 us (6%)
  local copies, waits for them, and re-layouts  28.8 us (6%)
  between operations  26.7 us (5%)
  starting transfers between devices  24.4 us (5%)
  other arithmetic  23.6 us (5%)
    psum x8, waiting for transfers between devices, body(): gram_sum = lax.psum(partial_value, 'row')  268 us
    psum x1, blocking collectives, body(): lax.psum((jnp.stack(off_list), jnp.stack(diag_list)), 'blk')  32.7 us
    ppermute x16, waiting for transfers between devices, passed_along(): return lax.ppermute(shard, axis, pairs)  30.5 us
    dot_general x64, matrix products, rotation(): jnp.dot(rotator.T, rotator, precision=HIGH, preferred_element_type=jnp.fl...  26 us
    ppermute x16, starting transfers between devices, passed_along(): return lax.ppermute(shard, axis, pairs)  23.6 us
    dot_general x64, matrix products, rotation(): jnp.dot(rotator, square, precision=HIGH, preferred_element_type=jnp.float32)  21 us
    gather x8, local copies, waits for them, and re-layouts, rotation(): diag_vals = jnp.diagonal(gram_sum)  15.5 us
    dot_general x8, matrix products, body(): jnp.dot(local_rows.T, local_rows, precision=HIGH, preferred_element_type=...  15.3 us
  transfers between devices with their start and end apart: 24, of which 22 were waited for; matrix products, arithmetic and copies ran while one was open for 2% of the time, Pallas kernels for 0%

commit v1 on v0

v1 whole, which is shorter than its diff:
```python
import functools

import jax
import jax.numpy as jnp
from jax import lax
from jax.experimental import pallas as pl
from jax.experimental.pallas import tpu as pltpu
from jax.sharding import PartitionSpec as P

ROUNDS = 8
NS_STEPS = 8
WIDTH = 512
MESH = pl.DeviceIdType.MESH
BF16 = jnp.bfloat16
F32 = jnp.float32


def split(x):
    hi = x.astype(BF16)
    lo = (x - hi.astype(F32)).astype(BF16)
    return hi, lo


def nn(a, b):
    return lax.dot_general(a, b, (((1,), (0,)), ((), ())), preferred_element_type=F32)


def nt(a, b):
    return lax.dot_general(a, b, (((1,), (1,)), ((), ())), preferred_element_type=F32)


def polar_step(v):
    n = v.shape[0]
    hi, lo = split(v)
    both = jnp.concatenate([hi, lo], axis=1)
    twice = jnp.concatenate(
        [jnp.concatenate([hi, hi], axis=1), jnp.concatenate([lo, lo], axis=1)], axis=0
    )
    square = nt(both, twice)
    square = square[:, :n] + square[:, n:]
    shi, slo = split(square)
    lines = jnp.concatenate([both, both], axis=0)
    turned = nn(jnp.concatenate([shi, slo], axis=1), lines)
    return 1.5 * v - 0.5 * (turned[:, :n] + turned[:, n:])


def kernel(
    n_row, n_blk, c_mat, c_all, width,
    mat_ref, pri_ref, turned_ref, trans_ref, stats_ref,
    frame, outgo, halves, grams,
    send_sem, recv_sem, gsend_sem, grecv_sem,
):
    me_row = lax.axis_index("row")
    me = lax.axis_index("blk")
    half = frame.shape[3]
    pair = 2 * half
    has_up = me < n_blk - 1
    has_down = me > 0
    is_first = me == 0
    is_last = me == n_blk - 1

    barrier = pltpu.get_barrier_semaphore()
    for d in range(1, n_row):
        pl.semaphore_signal(
            barrier, inc=1, device_id=(lax.rem(me_row + d, n_row), me), device_id_type=MESH
        )

    @pl.when(has_up)
    def _():
        pl.semaphore_signal(barrier, inc=1, device_id=(me_row, me + 1), device_id_type=MESH)

    @pl.when(has_down)
    def _():
        pl.semaphore_signal(barrier, inc=1, device_id=(me_row, me - 1), device_id_type=MESH)

    peers = n_row - 1 + jnp.where(has_up, 1, 0) + jnp.where(has_down, 1, 0)
    pl.semaphore_wait(barrier, peers)

    up_src = jnp.where(is_first, 1, 0)

    def up_copy(par, c):
        return pltpu.make_async_remote_copy(
            src_ref=outgo.at[up_src, c], dst_ref=frame.at[par, 0, c],
            send_sem=send_sem.at[0, c], recv_sem=recv_sem.at[par, 0, c],
            device_id=(me_row, me + 1), device_id_type=MESH,
        )

    def down_copy(par, c):
        return pltpu.make_async_remote_copy(
            src_ref=outgo.at[1, c], dst_ref=frame.at[par, 1, c],
            send_sem=send_sem.at[1, c], recv_sem=recv_sem.at[par, 1, c],
            device_id=(me_row, me - 1), device_id_type=MESH,
        )

    def wait_sent(c):
        @pl.when(has_up)
        def _():
            up_copy(0, c).wait_send()

        @pl.when(has_down)
        def _():
            down_copy(0, c).wait_send()

    def wait_arrived(par, c):
        @pl.when(has_down)
        def _():
            up_copy(par, c).wait_recv()

        @pl.when(has_up)
        def _():
            down_copy(par, c).wait_recv()

    def load_halves(par, c):
        t = jnp.concatenate([frame[par, 0, c], frame[par, 1, c]], axis=0)
        hi, lo = split(t)
        stack = jnp.concatenate([hi, lo], axis=0)
        halves[c] = stack
        return stack

    def gram_copy(par, d):
        return pltpu.make_async_remote_copy(
            src_ref=grams.at[par, me_row], dst_ref=grams.at[par, me_row],
            send_sem=gsend_sem.at[d - 1], recv_sem=grecv_sem.at[par, d - 1],
            device_id=(lax.rem(me_row + d, n_row), me), device_id_type=MESH,
        )

    for c in range(c_all):
        if c < c_mat:
            t = mat_ref[pl.ds(c * width, width), :].T
        else:
            t = pri_ref[pl.ds((c - c_mat) * width, width), :].T
        frame[0, 0, c] = t[:half]
        frame[0, 1, c] = t[half:]

    rows = lax.broadcasted_iota(jnp.int32, (pair, pair), 0)
    cols = lax.broadcasted_iota(jnp.int32, (pair, pair), 1)
    eye = rows == cols
    lean = (rows - cols).astype(F32) / pair
    identity = eye.astype(F32)

    def one_round(k, carry):
        par = lax.rem(k, 2)
        nxt = 1 - par
        gram = jnp.zeros((pair, pair), F32)
        for c in range(c_mat):
            @pl.when(k > 0)
            def _():
                wait_arrived(par, c)

            stack = load_halves(par, c)
            p4 = nt(stack, stack)
            p2 = p4[:pair] + p4[pair:]
            gram = gram + (p2[:, :pair] + p2[:, pair:])
        grams[par, me_row] = gram
        for d in range(1, n_row):
            gram_copy(par, d).start()
        for d in range(1, n_row):
            gram_copy(par, d).wait()
        gram = grams[par, 0]
        for r in range(1, n_row):
            gram = gram + grams[par, r]

        gram_sq = gram * gram
        mean_diag = jnp.sum(jnp.where(eye, gram, 0.0)) / pair
        off_sq = jnp.sum(jnp.where(eye, 0.0, gram_sq))
        diag_sq = jnp.sum(jnp.where(eye, gram_sq, 0.0))
        lane = lax.broadcasted_iota(jnp.int32, (1, stats_ref.shape[1]), 1)
        stats_ref[pl.ds(k, 1), :] = jnp.where(
            lane == 0, off_sq, jnp.where(lane == 1, diag_sq, 0.0)
        )
        skew = gram * lean / mean_diag
        factor = lax.rsqrt(jnp.full((1, pair), 1.0, F32) + jnp.sum(skew * skew))
        v = (identity + skew) * factor
        v = lax.fori_loop(0, NS_STEPS, lambda s, x: polar_step(x), v)
        vhi, vlo = split(v)
        left = jnp.concatenate(
            [jnp.concatenate([vhi, vhi], axis=1), jnp.concatenate([vlo, vlo], axis=1)], axis=0
        )

        for c in range(c_all):
            @pl.when(k > 0)
            def _():
                wait_sent(c)
                if c >= c_mat:
                    wait_arrived(par, c)

            stack = halves[c] if c < c_mat else load_halves(par, c)
            both = nn(left, stack)
            rotated = both[:pair] + both[pair:]
            outgo[0, c] = rotated[:half]
            outgo[1, c] = rotated[half:]

            @pl.when(has_up)
            def _():
                up_copy(nxt, c).start()

            @pl.when(has_down)
            def _():
                down_copy(nxt, c).start()

            @pl.when(is_first)
            def _():
                frame[nxt, 0, c] = rotated[:half]

            @pl.when(is_last)
            def _():
                frame[nxt, 1, c] = rotated[:half]

        return carry

    lax.fori_loop(0, ROUNDS, one_round, 0)

    last = ROUNDS % 2
    for c in range(c_all):
        wait_arrived(last, c)
        wait_sent(c)
        t = jnp.concatenate([frame[last, 0, c], frame[last, 1, c]], axis=0).T
        if c < c_mat:
            turned_ref[pl.ds(c * width, width), :] = t
        else:
            trans_ref[pl.ds((c - c_mat) * width, width), :] = t


def body(matrix, prior):
    n_row = lax.axis_size("row")
    n_blk = lax.axis_size("blk")
    pair = matrix.shape[1]
    half = pair // 2
    width = min(WIDTH, matrix.shape[0], prior.shape[0])
    c_mat = matrix.shape[0] // width
    c_all = c_mat + prior.shape[0] // width
    vmem = pl.BlockSpec(memory_space=pltpu.VMEM)
    turned, trans, stats = pl.pallas_call(
        functools.partial(kernel, n_row, n_blk, c_mat, c_all, width),
        out_shape=(
            jax.ShapeDtypeStruct(matrix.shape, F32),
            jax.ShapeDtypeStruct(prior.shape, F32),
            jax.ShapeDtypeStruct((ROUNDS, 128), F32),
        ),
        in_specs=[vmem, vmem],
        out_specs=(vmem, vmem, vmem),
        scratch_shapes=[
            pltpu.VMEM((2, 2, c_all, half, width), F32),
            pltpu.VMEM((2, c_all, half, width), F32),
            pltpu.VMEM((c_all, 2 * pair, width), BF16),
            pltpu.VMEM((2, n_row, pair, pair), F32),
            pltpu.SemaphoreType.DMA((2, c_all)),
            pltpu.SemaphoreType.DMA((2, 2, c_all)),
            pltpu.SemaphoreType.DMA((max(n_row - 1, 1),)),
            pltpu.SemaphoreType.DMA((2, max(n_row - 1, 1))),
        ],
        compiler_params=pltpu.CompilerParams(
            collective_id=0, has_side_effects=True, vmem_limit_bytes=40 * 1024 * 1024
        ),
    )(matrix, prior)
    sums = lax.psum(stats[:, :2], "blk")
    return turned, trans, jnp.sqrt(sums[:, 0] / sums[:, 1])


def solution(mesh):
    return jax.shard_map(
        body,
        mesh=mesh,
        in_specs=(P("row", "blk"), P("row", "blk")),
        out_specs=(P("row", "blk"), P("row", "blk"), P()),
        check_vma=False,
    )
```

time: 517 us -> 210 us (0.41); the launches traced: 509 us -> 210 us
  waiting for transfers between devices: 298 us -> 0 us
  Pallas kernels: 0 us -> 133 us
  matrix products: 74.7 us -> 0 us
  blocking collectives: 32.7 us -> 72.1 us
  between operations: 26.7 us -> 0.65 us
  local copies, waits for them, and re-layouts: 28.8 us -> 4.02 us
  starting transfers between devices: 24.4 us -> 0 us
  other arithmetic: 23.6 us -> 0.71 us
    psum x8 -> x0, waiting for transfers between devices: 268 us -> none  [body(): gram_sum = lax.psum(partial_value, 'row')]
    pallas_call x0 -> x1, Pallas kernels: none -> 133 us  [body(): pl.pallas_call(functools.partial(kernel, n_row, n_blk, c_mat, c_all, widt...]
    dot_general x144 -> x0, matrix products: 74.7 us -> none  [the longest x64 26 us: rotation(): jnp.dot(rotator.T, rotator, precision=HIGH, preferred_element_type=jnp.fl...]
    psum x1, blocking collectives: 32.7 us -> 72.1 us  [body(): sums = lax.psum(stats[:, :2], 'blk')]
    ppermute x16 -> x0, waiting for transfers between devices: 30.5 us -> none  [passed_along(): return lax.ppermute(shard, axis, pairs)]
    ppermute x16 -> x0, starting transfers between devices: 23.6 us -> none  [passed_along(): return lax.ppermute(shard, axis, pairs)]
    reduce_sum x16 -> x0, other arithmetic: 17.6 us -> none  [the longest x8 12.5 us: rotation(): off_sq = jnp.sum(jnp.where(identity > 0.5, 0.0, gram_sum * gram_sum))]
    gather x8 -> x0, local copies, waits for them, and re-layouts: 15.5 us -> none  [rotation(): diag_vals = jnp.diagonal(gram_sum)]
  transfers between devices with their start and end apart: 24 -> 0, of which waited for: 22 -> 0; matrix products, arithmetic and copies ran while one was open for 2% -> 0% of each run, Pallas kernels for 0% -> 0%
where the time goes in v1:
time: 210 us
  Pallas kernels  133 us (63%)
  blocking collectives  72.1 us (34%)
  local copies, waits for them, and re-layouts  4.02 us (2%)
    pallas_call x1, Pallas kernels, body(): pl.pallas_call(functools.partial(kernel, n_row, n_blk, c_mat, c_all, widt...  133 us
    psum x1, blocking collectives, body(): sums = lax.psum(stats[:, :2], 'blk')  72.1 us

profile of v1, /device:TPU:0, one launch (start us, length us, event | category | flops | bytes accessed | tf_op | source)
XLA Modules:
  0.0 210.2 jit_solution(8670669885542551022)
XLA Ops:
  0.6 0.0 copy-start
  0.6 1.2 copy-done
  1.9 0.0 copy-start.1
  1.9 1.0 copy-done.1
  2.9 132.7 %shard_map.49 = (f32[2048,128]{1,0:T(8,128)S(1)}, f32[1024,128]{1,0:T(8,128)S(1)}, f32[8,128]{1,0:T(8,128)S(1)}) custom-call(f32[2048,128]{1,0:T(8,128)S(1)} %copy-done, f32[1024,128]{1,0:T(8,128)S(1)} %copy-done.1), custom_call_target="tpu_custom_call" | custom-call | tf_op jit(solution)/shard_map/pallas_call | solution.py:233
  135.7 72.1 %psum.7 = f32[8,2]{1,0:T(8,128)S(1)} all-reduce(f32[8,2]{1,0:T(8,128)S(1)} %bitcast.1), channel_id=1, replica_groups=mesh['row'=2,'blk'=16] {'blk'}, use_global_device_ids=true, to_apply=%region_0.0 | all-reduce | flops 16 | bytes 128 | tf_op jit(solution)/shard_map/psum | solution.py:256
  207.7 0.7 sqrt_reduce_fusion
  208.5 1.0 copy.7
  209.4 0.8 copy.8
Async XLA Ops:
  0.6 1.2 copy-start
  1.9 1.0 copy-start.1

commit v2 on v1

v2 whole, which is shorter than its diff:
```python
import functools

import jax
import jax.numpy as jnp
from jax import lax
from jax.experimental import pallas as pl
from jax.experimental.pallas import tpu as pltpu
from jax.sharding import PartitionSpec as P

ROUNDS = 8
NS_STEPS = 8
WIDTH = 512
MESH = pl.DeviceIdType.MESH
BF16 = jnp.bfloat16
F32 = jnp.float32


def split(x):
    hi = x.astype(BF16)
    lo = (x - hi.astype(F32)).astype(BF16)
    return hi, lo


def nn(a, b):
    return lax.dot_general(a, b, (((1,), (0,)), ((), ())), preferred_element_type=F32)


def nt(a, b):
    return lax.dot_general(a, b, (((1,), (1,)), ((), ())), preferred_element_type=F32)


def polar_step(v):
    n = v.shape[0]
    hi, lo = split(v)
    both = jnp.concatenate([hi, lo], axis=1)
    twice = jnp.concatenate(
        [jnp.concatenate([hi, hi], axis=1), jnp.concatenate([lo, lo], axis=1)], axis=0
    )
    square = nt(both, twice)
    square = square[:, :n] + square[:, n:]
    shi, slo = split(square)
    lines = jnp.concatenate([both, both], axis=0)
    turned = nn(jnp.concatenate([shi, slo], axis=1), lines)
    return 1.5 * v - 0.5 * (turned[:, :n] + turned[:, n:])


def kernel(
    n_row, n_blk, c_mat, c_all, width, cores, side, doublings,
    mat_ref, pri_ref, turned_ref, trans_ref, stats_ref,
    frame, outgo, halves, grams, tallies,
    send_sem, recv_sem, gsend_sem, grecv_sem, ssend_sem, srecv_sem,
):
    me_row = lax.axis_index("row")
    me = lax.axis_index("blk")
    half = frame.shape[3]
    pair = 2 * half
    end = n_blk - 1
    final = ROUNDS - 1

    def place(p):
        chip = lax.div(p, cores)
        plane = lax.div(chip, side)
        spot = lax.rem(chip, side)
        spot = jnp.where(lax.rem(plane, 2) == 1, side - 1 - spot, spot)
        return (plane * side + spot) * cores + lax.rem(p, cores)

    mine = place(me)

    def above(p):
        return jnp.minimum(p + 1, end)

    def below(p):
        return jnp.maximum(p - 1, 0)

    def partner(j):
        step = 2 ** j
        return jnp.where(lax.rem(lax.div(me, step), 2) == 0, me + step, me - step)

    barrier = pltpu.get_barrier_semaphore()

    def greet(row, blk):
        pl.semaphore_signal(barrier, inc=1, device_id=(row, blk), device_id_type=MESH)

    peers = n_row - 1 + doublings
    for d in range(1, n_row):
        greet(lax.rem(me_row + d, n_row), me)
    for j in range(doublings):
        greet(me_row, partner(j))
    meets = [
        (mine < end, place(above(mine))), (mine > 0, place(below(mine))),
        (me < end, place(above(me))), (me > 0, place(below(me))),
        (mine < end, above(mine)), (mine > 0, below(mine)),
        ((me == end) & (mine != me), mine), ((mine == end) & (mine != me), mine),
    ]
    for on, blk in meets:
        @pl.when(on)
        def _():
            greet(me_row, blk)

        peers = peers + jnp.where(on, 1, 0)
    pl.semaphore_wait(barrier, peers)

    def slot_at(k):
        return jnp.where(k == 0, me, mine)

    def home_at(k, p):
        return jnp.where(k == final, p, place(p))

    def sends(k):
        s = slot_at(k)
        return (s < end) | (home_at(k, end) != me), s > 0

    def arrives(k):
        s = jnp.where(k == final + 1, me, mine)
        stays = jnp.where(k == 1, end == me, place(end) == me)
        return s > 0, (s < end) | jnp.logical_not(stays)

    def up_copy(k, par, c):
        s = slot_at(k)
        to = jnp.where(s == end, 1, 0)
        return pltpu.make_async_remote_copy(
            src_ref=outgo.at[jnp.where(s == 0, 1, 0), c], dst_ref=frame.at[par, to, c],
            send_sem=send_sem.at[0, c], recv_sem=recv_sem.at[par, to, c],
            device_id=(me_row, home_at(k, above(s))), device_id_type=MESH,
        )

    def down_copy(k, par, c):
        return pltpu.make_async_remote_copy(
            src_ref=outgo.at[1, c], dst_ref=frame.at[par, 1, c],
            send_sem=send_sem.at[1, c], recv_sem=recv_sem.at[par, 1, c],
            device_id=(me_row, home_at(k, below(slot_at(k)))), device_id_type=MESH,
        )

    def wait_sent(k, c):
        up_on, down_on = sends(k)

        @pl.when(up_on)
        def _():
            up_copy(k, 0, c).wait_send()

        @pl.when(down_on)
        def _():
            down_copy(k, 0, c).wait_send()

    def wait_arrived(k, par, c):
        for h, on in enumerate(arrives(k)):
            @pl.when(on)
            def _():
                pltpu.make_async_remote_copy(
                    src_ref=outgo.at[h, c], dst_ref=frame.at[par, h, c],
                    send_sem=send_sem.at[h, c], recv_sem=recv_sem.at[par, h, c],
                    device_id=(me_row, place(above(mine))), device_id_type=MESH,
                ).wait_recv()

    def load_halves(par, c):
        t = jnp.concatenate([frame[par, 0, c], frame[par, 1, c]], axis=0)
        hi, lo = split(t)
        stack = jnp.concatenate([hi, lo], axis=0)
        halves[c] = stack
        return stack

    def gram_copy(par, d):
        return pltpu.make_async_remote_copy(
            src_ref=grams.at[par, me_row], dst_ref=grams.at[par, me_row],
            send_sem=gsend_sem.at[d - 1], recv_sem=grecv_sem.at[par, d - 1],
            device_id=(lax.rem(me_row + d, n_row), me), device_id_type=MESH,
        )

    for c in range(c_all):
        if c < c_mat:
            t = mat_ref[pl.ds(c * width, width), :].T
        else:
            t = pri_ref[pl.ds((c - c_mat) * width, width), :].T
        frame[2, 0, c] = t[:half]
        frame[2, 1, c] = t[half:]

    rows = lax.broadcasted_iota(jnp.int32, (pair, pair), 0)
    cols = lax.broadcasted_iota(jnp.int32, (pair, pair), 1)
    eye = rows == cols
    lean = (rows - cols).astype(F32) / pair
    identity = eye.astype(F32)

    def one_round(k, carry):
        even = lax.rem(k, 2)
        par = jnp.where(k == 0, 2, even)
        nxt = jnp.where(k == final, 2, 1 - even)
        s = slot_at(k)
        up_on, down_on = sends(k)
        gram = jnp.zeros((pair, pair), F32)
        for c in range(c_mat):
            @pl.when(k > 0)
            def _():
                wait_arrived(k, par, c)

            stack = load_halves(par, c)
            p4 = nt(stack, stack)
            p2 = p4[:pair] + p4[pair:]
            gram = gram + (p2[:, :pair] + p2[:, pair:])
        grams[even, me_row] = gram
        for d in range(1, n_row):
            gram_copy(even, d).start()
        for d in range(1, n_row):
            gram_copy(even, d).wait()
        gram = grams[even, 0]
        for r in range(1, n_row):
            gram = gram + grams[even, r]

        gram_sq = gram * gram
        mean_diag = jnp.sum(jnp.where(eye, gram, 0.0)) / pair
        off_sq = jnp.sum(jnp.where(eye, 0.0, gram_sq))
        diag_sq = jnp.sum(jnp.where(eye, gram_sq, 0.0))
        lane = lax.broadcasted_iota(jnp.int32, (1, stats_ref.shape[1]), 1)
        tallies[0, pl.ds(k, 1), :] = jnp.where(
            lane == 0, off_sq, jnp.where(lane == 1, diag_sq, 0.0)
        )
        skew = gram * lean / mean_diag
        factor = lax.rsqrt(jnp.full((1, pair), 1.0, F32) + jnp.sum(skew * skew))
        v = (identity + skew) * factor
        v = lax.fori_loop(0, NS_STEPS, lambda s, x: polar_step(x), v)
        vhi, vlo = split(v)
        left = jnp.concatenate(
            [jnp.concatenate([vhi, vhi], axis=1), jnp.concatenate([vlo, vlo], axis=1)], axis=0
        )

        for c in range(c_all):
            @pl.when(k > 0)
            def _():
                wait_sent(k - 1, c)
                if c >= c_mat:
                    wait_arrived(k, par, c)

            stack = halves[c] if c < c_mat else load_halves(par, c)
            both = nn(left, stack)
            rotated = both[:pair] + both[pair:]
            outgo[0, c] = rotated[:half]
            outgo[1, c] = rotated[half:]

            @pl.when(up_on)
            def _():
                up_copy(k, nxt, c).start()

            @pl.when(down_on)
            def _():
                down_copy(k, nxt, c).start()

            @pl.when(s == 0)
            def _():
                frame[nxt, 0, c] = rotated[:half]

            @pl.when((s == end) & jnp.logical_not(up_on))
            def _():
                frame[nxt, 1, c] = rotated[:half]

        return carry

    lax.fori_loop(0, ROUNDS, one_round, 0)

    for j in range(doublings):
        copy = pltpu.make_async_remote_copy(
            src_ref=tallies.at[2 * j], dst_ref=tallies.at[2 * j + 1],
            send_sem=ssend_sem.at[j], recv_sem=srecv_sem.at[j],
            device_id=(me_row, partner(j)), device_id_type=MESH,
        )
        copy.start()
        copy.wait()
        tallies[2 * j + 2] = tallies[2 * j] + tallies[2 * j + 1]
    stats_ref[...] = tallies[2 * doublings]

    for c in range(c_all):
        wait_arrived(final + 1, 2, c)
        wait_sent(final, c)
        t = jnp.concatenate([frame[2, 0, c], frame[2, 1, c]], axis=0).T
        if c < c_mat:
            turned_ref[pl.ds(c * width, width), :] = t
        else:
            trans_ref[pl.ds((c - c_mat) * width, width), :] = t


def body(cores, side, matrix, prior):
    n_row = lax.axis_size("row")
    n_blk = lax.axis_size("blk")
    pair = matrix.shape[1]
    half = pair // 2
    width = min(WIDTH, matrix.shape[0], prior.shape[0])
    c_mat = matrix.shape[0] // width
    c_all = c_mat + prior.shape[0] // width
    doublings = n_blk.bit_length() - 1
    if 2**doublings != n_blk:
        doublings = 0
    vmem = pl.BlockSpec(memory_space=pltpu.VMEM)
    turned, trans, stats = pl.pallas_call(
        functools.partial(kernel, n_row, n_blk, c_mat, c_all, width, cores, side, doublings),
        out_shape=(
            jax.ShapeDtypeStruct(matrix.shape, F32),
            jax.ShapeDtypeStruct(prior.shape, F32),
            jax.ShapeDtypeStruct((ROUNDS, 128), F32),
        ),
        in_specs=[vmem, vmem],
        out_specs=(vmem, vmem, vmem),
        scratch_shapes=[
            pltpu.VMEM((3, 2, c_all, half, width), F32),
            pltpu.VMEM((2, c_all, half, width), F32),
            pltpu.VMEM((c_all, 2 * pair, width), BF16),
            pltpu.VMEM((2, n_row, pair, pair), F32),
            pltpu.VMEM((2 * doublings + 1, ROUNDS, 128), F32),
            pltpu.SemaphoreType.DMA((2, c_all)),
            pltpu.SemaphoreType.DMA((3, 2, c_all)),
            pltpu.SemaphoreType.DMA((max(n_row - 1, 1),)),
            pltpu.SemaphoreType.DMA((2, max(n_row - 1, 1))),
            pltpu.SemaphoreType.DMA((max(doublings, 1),)),
            pltpu.SemaphoreType.DMA((max(doublings, 1),)),
        ],
        compiler_params=pltpu.CompilerParams(
            collective_id=0, has_side_effects=True, vmem_limit_bytes=40 * 1024 * 1024
        ),
    )(matrix, prior)
    sums = stats[:, :2]
    if not doublings:
        sums = lax.psum(sums, "blk")
    return turned, trans, jnp.sqrt(sums[:, 0] / sums[:, 1])


def layout(mesh):
    coords = [tuple(getattr(d, "coords", None) or (0,)) for d in mesh.devices[0]]
    n = len(coords)
    cores = 1
    while cores < n and coords[cores] == coords[0]:
        cores += 1
    if n % cores:
        return 1, n
    chips = coords[::cores]
    side = 1
    while side < len(chips) and sum(abs(p - q) for p, q in zip(chips[side], chips[side - 1])) == 1:
        side += 1
    if len(chips) % side:
        side = len(chips)
    return cores, side


def solution(mesh):
    return jax.shard_map(
        functools.partial(body, *layout(mesh)),
        mesh=mesh,
        in_specs=(P("row", "blk"), P("row", "blk")),
        out_specs=(P("row", "blk"), P("row", "blk"), P()),
        check_vma=False,
    )
```

time: 210 us -> 159 us (0.76)
  blocking collectives: 72.1 us -> 0 us
  Pallas kernels: 133 us -> 154 us
    psum x1 -> x0, blocking collectives: 72.1 us -> none  [body(): sums = lax.psum(stats[:, :2], 'blk')]
    pallas_call x1, Pallas kernels: 133 us -> 154 us  [body(): pl.pallas_call(functools.partial(kernel, n_row, n_blk, c_mat, c_all, widt...]
where the time goes in v2:
time: 159 us
  Pallas kernels  154 us (97%)
  local copies, waits for them, and re-layouts  4.02 us (3%)
    pallas_call x1, Pallas kernels, body(): pl.pallas_call(functools.partial(kernel, n_row, n_blk, c_mat, c_all, widt...  154 us
    unnamed x6, local copies, waits for them, and re-layouts  4.02 us

profile of v2, /device:TPU:0, one launch (start us, length us, event | category | flops | bytes accessed | tf_op | source)
XLA Modules:
  0.0 159.2 jit_solution(7630509447148274053)
XLA Ops:
  0.6 0.0 copy-start
  0.6 1.2 copy-done
  1.9 0.0 copy-start.1
  1.9 1.0 copy-done.1
  2.9 153.8 %shard_map.49 = (f32[2048,128]{1,0:T(8,128)S(1)}, f32[1024,128]{1,0:T(8,128)S(1)}, f32[8,128]{1,0:T(8,128)S(1)}) custom-call(f32[2048,128]{1,0:T(8,128)S(1)} %copy-done, f32[1024,128]{1,0:T(8,128)S(1)} %copy-done.1), custom_call_target="tpu_custom_call" | custom-call | tf_op jit(solution)/shard_map/pallas_call | solution.py:291
  156.7 0.7 sqrt_reduce_fusion
  157.4 1.0 copy.7
  158.4 0.8 copy.8
Async XLA Ops:
  0.6 1.2 copy-start
  1.9 1.0 copy-start.1

commit v3 on v2

--- a/solution.py
+++ b/solution.py
@@ -320,26 +320,9 @@
     return turned, trans, jnp.sqrt(sums[:, 0] / sums[:, 1])
 
 
-def layout(mesh):
-    coords = [tuple(getattr(d, "coords", None) or (0,)) for d in mesh.devices[0]]
-    n = len(coords)
-    cores = 1
-    while cores < n and coords[cores] == coords[0]:
-        cores += 1
-    if n % cores:
-        return 1, n
-    chips = coords[::cores]
-    side = 1
-    while side < len(chips) and sum(abs(p - q) for p, q in zip(chips[side], chips[side - 1])) == 1:
-        side += 1
-    if len(chips) % side:
-        side = len(chips)
-    return cores, side
-
-
 def solution(mesh):
     return jax.shard_map(
-        functools.partial(body, *layout(mesh)),
+        functools.partial(body, 1, mesh.shape["blk"]),
         mesh=mesh,
         in_specs=(P("row", "blk"), P("row", "blk")),
         out_specs=(P("row", "blk"), P("row", "blk"), P()),

time: 159 us -> 163 us (1.025)
  Pallas kernels: 154 us -> 157 us
    pallas_call x1, Pallas kernels: 154 us -> 157 us  [body(): pl.pallas_call(functools.partial(kernel, n_row, n_blk, c_mat, c_all, widt...]
where the time goes in v3:
time: 163 us
  Pallas kernels  157 us (96%)
  local copies, waits for them, and re-layouts  4.02 us (2%)
    pallas_call x1, Pallas kernels, body(): pl.pallas_call(functools.partial(kernel, n_row, n_blk, c_mat, c_all, widt...  157 us
    unnamed x6, local copies, waits for them, and re-layouts  4.02 us

profile of v3, /device:TPU:0, one launch (start us, length us, event | category | flops | bytes accessed | tf_op | source)
XLA Modules:
  0.0 162.7 jit_solution(306375792232920651)
XLA Ops:
  0.6 0.0 copy-start
  0.6 1.2 copy-done
  1.9 0.0 copy-start.1
  1.9 1.0 copy-done.1
  2.9 157.3 %shard_map.49 = (f32[2048,128]{1,0:T(8,128)S(1)}, f32[1024,128]{1,0:T(8,128)S(1)}, f32[8,128]{1,0:T(8,128)S(1)}) custom-call(f32[2048,128]{1,0:T(8,128)S(1)} %copy-done, f32[1024,128]{1,0:T(8,128)S(1)} %copy-done.1), custom_call_target="tpu_custom_call" | custom-call | tf_op jit(solution)/shard_map/pallas_call | solution.py:291
  160.2 0.7 sqrt_reduce_fusion
  161.0 1.0 copy.7
  161.9 0.8 copy.8
Async XLA Ops:
  0.6 1.2 copy-start
  1.9 1.0 copy-start.1

commit v4 on v3

--- a/solution.py
+++ b/solution.py
@@ -9,7 +9,7 @@
 
 ROUNDS = 8
 NS_STEPS = 8
-WIDTH = 512
+WIDTH = 256
 MESH = pl.DeviceIdType.MESH
 BF16 = jnp.bfloat16
 F32 = jnp.float32
@@ -45,9 +45,9 @@
 
 
 def kernel(
-    n_row, n_blk, c_mat, c_all, width, cores, side, doublings,
+    n_row, n_blk, c_mat, c_all, width, cores, side, group,
     mat_ref, pri_ref, turned_ref, trans_ref, stats_ref,
-    frame, outgo, halves, grams, tallies,
+    frame, outgo, halves, grams, tally, near, far,
     send_sem, recv_sem, gsend_sem, grecv_sem, ssend_sem, srecv_sem,
 ):
     me_row = lax.axis_index("row")
@@ -72,20 +72,43 @@
     def below(p):
         return jnp.maximum(p - 1, 0)
 
-    def partner(j):
-        step = 2 ** j
-        return jnp.where(lax.rem(lax.div(me, step), 2) == 0, me + step, me - step)
+    groups = n_blk // group
+    in_group = lax.rem(me, group)
+    my_group = lax.div(me, group)
+
+    def near_peer(d):
+        return my_group * group + lax.rem(in_group + d, group)
+
+    def far_peer(d):
+        return lax.rem(my_group + d, groups) * group + in_group
+
+    def near_copy(d):
+        return pltpu.make_async_remote_copy(
+            src_ref=near.at[in_group], dst_ref=near.at[in_group],
+            send_sem=ssend_sem.at[d - 1], recv_sem=srecv_sem.at[d - 1],
+            device_id=(me_row, near_peer(d)), device_id_type=MESH,
+        )
+
+    def far_copy(d):
+        sem = group + d - 2
+        return pltpu.make_async_remote_copy(
+            src_ref=far.at[my_group], dst_ref=far.at[my_group],
+            send_sem=ssend_sem.at[sem], recv_sem=srecv_sem.at[sem],
+            device_id=(me_row, far_peer(d)), device_id_type=MESH,
+        )
 
     barrier = pltpu.get_barrier_semaphore()
 
     def greet(row, blk):
         pl.semaphore_signal(barrier, inc=1, device_id=(row, blk), device_id_type=MESH)
 
-    peers = n_row - 1 + doublings
+    peers = n_row - 1 + group - 1 + groups - 1
     for d in range(1, n_row):
         greet(lax.rem(me_row + d, n_row), me)
-    for j in range(doublings):
-        greet(me_row, partner(j))
+    for d in range(1, group):
+        greet(me_row, near_peer(d))
+    for d in range(1, groups):
+        greet(me_row, far_peer(d))
     meets = [
         (mine < end, place(above(mine))), (mine > 0, place(below(mine))),
         (me < end, place(above(me))), (me > 0, place(below(me))),
@@ -166,13 +189,13 @@
             device_id=(lax.rem(me_row + d, n_row), me), device_id_type=MESH,
         )
 
-    for c in range(c_all):
-        if c < c_mat:
-            t = mat_ref[pl.ds(c * width, width), :].T
-        else:
-            t = pri_ref[pl.ds((c - c_mat) * width, width), :].T
+    def bring(ref, c, first):
+        t = ref[pl.ds((c - first) * width, width), :].T
         frame[2, 0, c] = t[:half]
         frame[2, 1, c] = t[half:]
+
+    for c in range(c_mat):
+        bring(mat_ref, c, 0)
 
     rows = lax.broadcasted_iota(jnp.int32, (pair, pair), 0)
     cols = lax.broadcasted_iota(jnp.int32, (pair, pair), 1)
@@ -199,6 +222,12 @@
         grams[even, me_row] = gram
         for d in range(1, n_row):
             gram_copy(even, d).start()
+
+        @pl.when(k == 0)
+        def _():
+            for c in range(c_mat, c_all):
+                bring(pri_ref, c, c_mat)
+
         for d in range(1, n_row):
             gram_copy(even, d).wait()
         gram = grams[even, 0]
@@ -210,13 +239,32 @@
         off_sq = jnp.sum(jnp.where(eye, 0.0, gram_sq))
         diag_sq = jnp.sum(jnp.where(eye, gram_sq, 0.0))
         lane = lax.broadcasted_iota(jnp.int32, (1, stats_ref.shape[1]), 1)
-        tallies[0, pl.ds(k, 1), :] = jnp.where(
+        tally[pl.ds(k, 1), :] = jnp.where(
             lane == 0, off_sq, jnp.where(lane == 1, diag_sq, 0.0)
         )
+
+        @pl.when(k == final)
+        def _():
+            near[in_group] = tally[...]
+            for d in range(1, group):
+                near_copy(d).start()
+
         skew = gram * lean / mean_diag
         factor = lax.rsqrt(jnp.full((1, pair), 1.0, F32) + jnp.sum(skew * skew))
         v = (identity + skew) * factor
         v = lax.fori_loop(0, NS_STEPS, lambda s, x: polar_step(x), v)
+
+        @pl.when(k == final)
+        def _():
+            for d in range(1, group):
+                near_copy(d).wait()
+            total = near[0]
+            for r in range(1, group):
+                total = total + near[r]
+            far[my_group] = total
+            for d in range(1, groups):
+                far_copy(d).start()
+
         vhi, vlo = split(v)
         left = jnp.concatenate(
             [jnp.concatenate([vhi, vhi], axis=1), jnp.concatenate([vlo, vlo], axis=1)], axis=0
@@ -255,16 +303,12 @@
 
     lax.fori_loop(0, ROUNDS, one_round, 0)
 
-    for j in range(doublings):
-        copy = pltpu.make_async_remote_copy(
-            src_ref=tallies.at[2 * j], dst_ref=tallies.at[2 * j + 1],
-            send_sem=ssend_sem.at[j], recv_sem=srecv_sem.at[j],
-            device_id=(me_row, partner(j)), device_id_type=MESH,
-        )
-        copy.start()
-        copy.wait()
-        tallies[2 * j + 2] = tallies[2 * j] + tallies[2 * j + 1]
-    stats_ref[...] = tallies[2 * doublings]
+    for d in range(1, groups):
+        far_copy(d).wait()
+    total = far[0]
+    for r in range(1, groups):
+        total = total + far[r]
+    stats_ref[...] = total
 
     for c in range(c_all):
         wait_arrived(final + 1, 2, c)
@@ -284,12 +328,11 @@
     width = min(WIDTH, matrix.shape[0], prior.shape[0])
     c_mat = matrix.shape[0] // width
     c_all = c_mat + prior.shape[0] // width
-    doublings = n_blk.bit_length() - 1
-    if 2**doublings != n_blk:
-        doublings = 0
+    group = max(g for g in range(1, n_blk + 1) if n_blk % g == 0 and g * g <= n_blk)
+    sums_sent = max(group + n_blk // group - 2, 1)
     vmem = pl.BlockSpec(memory_space=pltpu.VMEM)
     turned, trans, stats = pl.pallas_call(
-        functools.partial(kernel, n_row, n_blk, c_mat, c_all, width, cores, side, doublings),
+        functools.partial(kernel, n_row, n_blk, c_mat, c_all, width, cores, side, group),
         out_shape=(
             jax.ShapeDtypeStruct(matrix.shape, F32),
             jax.ShapeDtypeStruct(prior.shape, F32),
@@ -302,22 +345,21 @@
             pltpu.VMEM((2, c_all, half, width), F32),
             pltpu.VMEM((c_all, 2 * pair, width), BF16),
             pltpu.VMEM((2, n_row, pair, pair), F32),
-            pltpu.VMEM((2 * doublings + 1, ROUNDS, 128), F32),
+            pltpu.VMEM((ROUNDS, 128), F32),
+            pltpu.VMEM((group, ROUNDS, 128), F32),
+            pltpu.VMEM((n_blk // group, ROUNDS, 128), F32),
             pltpu.SemaphoreType.DMA((2, c_all)),
             pltpu.SemaphoreType.DMA((3, 2, c_all)),
             pltpu.SemaphoreType.DMA((max(n_row - 1, 1),)),
             pltpu.SemaphoreType.DMA((2, max(n_row - 1, 1))),
-            pltpu.SemaphoreType.DMA((max(doublings, 1),)),
-            pltpu.SemaphoreType.DMA((max(doublings, 1),)),
+            pltpu.SemaphoreType.DMA((sums_sent,)),
+            pltpu.SemaphoreType.DMA((sums_sent,)),
         ],
         compiler_params=pltpu.CompilerParams(
             collective_id=0, has_side_effects=True, vmem_limit_bytes=40 * 1024 * 1024
         ),
     )(matrix, prior)
-    sums = stats[:, :2]
-    if not doublings:
-        sums = lax.psum(sums, "blk")
-    return turned, trans, jnp.sqrt(sums[:, 0] / sums[:, 1])
+    return turned, trans, jnp.sqrt(stats[:, 0] / stats[:, 1])
 
 
 def solution(mesh):

time: 163 us -> 160 us (0.982)
  the two profiles are of different devices: /device:TPU:0 before, /device:TPU:1 now
where the time goes in v4:
time: 160 us
  Pallas kernels  154 us (96%)
  local copies, waits for them, and re-layouts  4.02 us (3%)
    pallas_call x1, Pallas kernels, body(): pl.pallas_call(functools.partial(kernel, n_row, n_blk, c_mat, c_all, widt...  154 us
    unnamed x6, local copies, waits for them, and re-layouts  4.02 us

profile of v4, /device:TPU:1, one launch (start us, length us, event | category | flops | bytes accessed | tf_op | source)
XLA Modules:
  0.0 159.7 jit_solution(4545870070355802701)
XLA Ops:
  0.6 0.0 copy-start
  0.6 1.2 copy-done
  1.9 0.0 copy-start.1
  1.9 1.0 copy-done.1
  2.9 154.3 %shard_map.49 = (f32[2048,128]{1,0:T(8,128)S(1)}, f32[1024,128]{1,0:T(8,128)S(1)}, f32[8,128]{1,0:T(8,128)S(1)}) custom-call(f32[2048,128]{1,0:T(8,128)S(1)} %copy-done, f32[1024,128]{1,0:T(8,128)S(1)} %copy-done.1), custom_call_target="tpu_custom_call" | custom-call | tf_op jit(solution)/shard_map/pallas_call | solution.py:334
  157.2 0.7 sqrt_reduce_fusion
  157.9 1.0 copy.7
  158.9 0.8 copy.8
Async XLA Ops:
  0.6 1.2 copy-start
  1.9 1.0 copy-start.1
